TPU v7x, 32 devices: a whole 2x2x4 slice. The times are simulated.
32 devices in a mesh: ctx: 16 (over z, y, x), vid: 2 (over core).
Axes of the slice: x: 2, y: 2, z: 4, core: 2. Of those that a mesh axis runs over, the one named last changes fastest.
Arguments:
- features: bfloat16 [2, 32, 8, 32, 256], P('vid', 'ctx'), may hold values from -6 to 6
- grad_out: bfloat16 [2, 32, 8, 32, 128], P('vid', 'ctx'), may hold values from -6 to 6
- mean_saved: float32 [2, 32], P('vid'), may hold values from -3 to 3
- rstd_saved: float32 [2, 32], P('vid'), may hold values from 0.5 to 2
- latent: float32 [2, 8, 16, 16], P('vid'), may hold values from -6 to 6
- gamma: float32 [256], replicated, may hold values from 0.5 to 1.5
- beta: float32 [256], replicated, may hold values from -3 to 3
- w_scale: float32 [16, 256], replicated, may hold values from -1.5 to 1.5
- b_scale: float32 [256], replicated, may hold values from -3 to 3
- w_shift: float32 [16, 256], replicated, may hold values from -1.5 to 1.5
- b_shift: float32 [256], replicated, may hold values from -3 to 3
- kernel: bfloat16 [6912, 128], replicated, may hold values from -0.078125 to 0.078125
Outputs:
- features_grad: bfloat16 [2, 32, 8, 32, 256], P('vid', 'ctx')
- kernel_grad: float32 [6912, 128], P('ctx', 'vid')
- mod_grads: float32 [2, 16, 256], replicated
- vector_grads: float32 [4, 256], replicated
- latent_grad: float32 [2, 16, 16, 8], P('vid', 'ctx')
All inputs are finite; a program needn't handle non-finite values.
Results may differ from a plain program's by a relative error of at most 0.0029.
Values may be sent and summed in bfloat16 or wider, within the bound.
No kernel may reach another device: no remote copies, remote signals or barrier semaphores. Data moves between devices by JAX's collectives and lax.ppermute only.
A program may use at most 64 MiB of HBM per device.

v0:
```python
import functools
import math

import jax
import jax.numpy as jnp
from jax import lax
from jax.experimental import pallas as pl
from jax.experimental.pallas import tpu as pltpu
from jax.sharding import PartitionSpec as P

NEAR = 4
CELL = 4
TAPS = 3
TILE = 16

f32 = jnp.float32
bf16 = jnp.bfloat16
dot = functools.partial(lax.dot_general, preferred_element_type=f32)
exact = functools.partial(dot, precision=lax.Precision.HIGHEST)
ROWS_COLS = (((1,), (0,)), ((), ()))
ROWS_ROWS = (((1,), (1,)), ((), ()))
COLS_COLS = (((0,), (0,)), ((), ()))


def call(body, outs, scratch=(), name=None, far_args=()):
    def run(*args):
        args = [pltpu.with_memory_space_constraint(arg, pltpu.HBM) if k in far_args else arg
                for k, arg in enumerate(args)]

        def full(*refs):
            refs = list(refs)
            sems = refs.pop()
            buffers = [refs.pop() for _ in far_args][::-1]
            moves = [pltpu.make_async_copy(refs[at], buffer, sems.at[k])
                     for k, (at, buffer) in enumerate(zip(far_args, buffers))]
            for move in moves:
                move.start()
            for at, buffer in zip(far_args, buffers):
                refs[at] = buffer
            for move in moves:
                move.wait()
            body(*refs)

        return pl.pallas_call(
            full if far_args else body,
            out_shape=outs,
            in_specs=[pl.BlockSpec(memory_space=pltpu.HBM if k in far_args else pltpu.VMEM) for k in range(len(args))],
            scratch_shapes=list(scratch) + [pltpu.VMEM(args[k].shape, args[k].dtype) for k in far_args]
            + ([pltpu.SemaphoreType.DMA((len(far_args),))] if far_args else []),
            name=name,
            compiler_params=pltpu.CompilerParams(vmem_limit_bytes=50 * 2**20),
        )(*args)

    return run


def halves(value):
    top = value.astype(bf16)
    return top, (value - top.astype(f32)).astype(bf16)


def shaped(shape, kind=f32):
    return jax.ShapeDtypeStruct(shape, kind)


def paired(place, turn, size):
    return place ^ turn if size & (size - 1) == 0 else (place + turn) % size


def cell_matrix(height, width, cells):
    pixel = lax.broadcasted_iota(jnp.int32, (height * width, cells), 0)
    cell = lax.broadcasted_iota(jnp.int32, (height * width, cells), 1)
    place = (pixel // width) // CELL * (width // CELL) + pixel % width // CELL
    return jnp.where(place == cell, 1.0, 0.0).astype(f32)


def modulate_body(frames, height, width, feats, mean, rstd, latent, gamma, beta, ws, bs, wt, bt,
                  act_t, slope, normed_out, gain_out, tab_out):
    chans = feats.shape[1]
    groups = mean.shape[1]
    pixels = height * width
    lat = latent[0, lax.axis_index("ctx") * frames // CELL]
    group = lax.broadcasted_iota(jnp.int32, (groups, chans), 0)
    chan = lax.broadcasted_iota(jnp.int32, (groups, chans), 1)
    member = jnp.where(chan // (chans // groups) == group, 1.0, 0.0).astype(f32)
    mean_chan = exact(mean[...], member, ROWS_COLS)
    rstd_chan = exact(rstd[...], member, ROWS_COLS)
    scale_tab = exact(lat, ws[...], COLS_COLS) + bs[...]
    shift_tab = exact(lat, wt[...], COLS_COLS) + bt[...]
    tab_out[...] = scale_tab
    cells = cell_matrix(height, width, lat.shape[1])
    scale_map = exact(cells, scale_tab, ROWS_COLS)
    shift_map = exact(cells, shift_tab, ROWS_COLS)
    gain_out[...] = scale_map * (gamma[...] * rstd_chan)
    for frame in range(frames):
        at = pl.ds(frame * pixels, pixels)
        normed = (feats[at, :].astype(f32) - mean_chan) * rstd_chan
        modulated = (normed * gamma[...] + beta[...]) * scale_map + shift_map
        squashed = jax.nn.sigmoid(modulated)
        normed_out[at, :] = normed
        slope[at, :] = squashed * (1.0 + modulated * (1.0 - squashed))
        act_t[:, at] = (modulated * squashed).T.astype(bf16)


def column_shifts(value, width):
    column = lax.broadcasted_iota(jnp.int32, value.shape, 0) % width
    rows = value.shape[0]
    return (
        jnp.where(column == width - 1, 0.0, pltpu.roll(value, rows - 1, 0)),
        value,
        jnp.where(column == 0, 0.0, pltpu.roll(value, 1, 0)),
    )


def clear_borders(padded, width):
    lead = padded.shape[:-2]
    length, lanes = padded.shape[-2:]
    edge = jnp.zeros(lead + (width, lanes), padded.dtype)
    every = (slice(None),) * len(lead)
    padded[every + (slice(0, width),)] = edge
    padded[every + (slice(length - width, length),)] = edge


def input_grad_body(frames, height, width, grads, beyond, weights, slope, normed, gain, tab, latent,
                    ws, wt, gamma, beta, feats_grad, small, lat_own, lat_far, shifted, total):
    pixels = height * width
    chans = gain.shape[1]
    device = lax.axis_index("ctx")
    clear_borders(shifted, width)
    for half, source in enumerate((grads, beyond)):
        for col, value in enumerate(column_shifts(source[...].astype(f32), width)):
            for frame in range(frames):
                shifted[col, half * frames + frame, width:width + pixels] = (
                    value[frame * pixels:(frame + 1) * pixels].astype(bf16))

    def window(frame, row, col):
        start = (TAPS - 1 - row) * width
        return shifted[col, frame, start:start + pixels]

    def filters(step):
        return jnp.concatenate(
            [weights[(step * TAPS * TAPS + k) * chans:(step * TAPS * TAPS + k + 1) * chans, :]
             for k in range(TAPS * TAPS)], axis=1)

    def windows(frame_list):
        return jnp.concatenate(
            [jnp.concatenate([window(frame, k // TAPS, k % TAPS) for k in range(TAPS * TAPS)], axis=1)
             for frame in frame_list], axis=0)

    for step in range(TAPS):
        term = dot(windows([t + TAPS - 1 - step for t in range(frames)]), filters(step), ROWS_ROWS)
        total[...] = term if step == 0 else total[...] + term

    @pl.when(device == 0)
    def _():
        for step in range(TAPS - 1):
            for frame in range(TAPS - 1 - step):
                total[0:pixels] += dot(windows([frame]), filters(step), ROWS_ROWS)

    pooled_shift = jnp.zeros((pixels, chans), f32)
    pooled_norm = jnp.zeros((pixels, chans), f32)
    for frame in range(frames):
        at = pl.ds(frame * pixels, pixels)
        pre = total[at, :] * slope[at, :]
        feats_grad[at, :] = (pre * gain[...]).astype(bf16)
        pooled_shift += pre
        pooled_norm += pre * normed[at, :]
    lat = latent[0, device * frames // CELL]
    depth, length = lat.shape
    cells = cell_matrix(height, width, length)
    shift_pool = exact(cells, pooled_shift, COLS_COLS)
    norm_pool = exact(cells, pooled_norm, COLS_COLS)
    scale_pool = norm_pool * gamma[...] + shift_pool * beta[...]
    small[0:depth] = exact(lat, scale_pool, ROWS_COLS)
    small[depth:2 * depth] = exact(lat, shift_pool, ROWS_COLS)
    for row, field in enumerate((norm_pool * tab[...], shift_pool * tab[...], scale_pool, shift_pool)):
        small[2 * depth + row:2 * depth + row + 1] = jnp.sum(field, axis=0, keepdims=True)
    latent_sum = exact(scale_pool, ws[...], ROWS_ROWS) + exact(shift_pool, wt[...], ROWS_ROWS)
    first, second = latent_sum[:length // 2], latent_sum[length // 2:]
    even = device % 2 == 0
    lat_own[...] = jnp.where(even, first, second)
    lat_far[...] = jnp.where(even, second, first)


def filter_grad_body(frames, height, width, videos, near, piece, *refs):
    acts, refs = refs[:videos], refs[videos:]
    grads, refs = refs[:videos], refs[videos:]
    beyond, refs = refs[:videos], refs[videos:]
    smalls, refs = refs[:videos], refs[videos:]
    lat_far, own, refs = refs[0], refs[1], refs[2:]
    sends, small_out, packs, blocks = refs[:near - 1], refs[near - 1], refs[near], refs[near + 1]
    pixels = height * width
    chans = acts[0].shape[0]
    lanes = grads[0].shape[1]
    cols = lanes // videos
    device = lax.axis_index("ctx")
    here = lax.axis_index("vid")
    per = min(videos, TAPS)
    banks = -(-TAPS // per)
    lane = lax.broadcasted_iota(jnp.int32, (1, lanes), 1)
    small = functools.reduce(lambda a, b: a + b, [ref[...] for ref in smalls])
    small_out[...] = jnp.zeros_like(small_out)
    for k in range(chans // lanes):
        small_out[k * small.shape[0]:(k + 1) * small.shape[0]] = small[:, k * lanes:(k + 1) * lanes]

    clear_borders(packs, width)
    for video in range(videos):
        for half, source in enumerate((grads[video], beyond[video])):
            value = pltpu.roll(source[...].astype(f32), lax.rem(lanes - here * cols, lanes), 1)
            moved = column_shifts(value, width)
            for bank in range(banks):
                packed = moved[bank * per]
                for k in range(1, min(per, TAPS - bank * per)):
                    packed = jnp.where(lane >= k * cols, pltpu.roll(moved[bank * per + k], k * cols, 1), packed)
                packed = packed.astype(bf16)
                for frame in range(frames):
                    packs[video, bank, half * frames + frame, width:width + pixels] = (
                        packed[frame * pixels:(frame + 1) * pixels])

    def window(video, frame, row, bank):
        start = (TAPS - 1 - row) * width
        return packs[video, bank, frame, start:start + pixels]

    slots = [(row, bank) for row in range(TAPS) for bank in range(banks)]

    def windows(video, frame):
        return jnp.concatenate([window(video, frame, row, bank) for row, bank in slots], axis=1)

    far, rows = blocks.shape[0], TAPS**3 * chans // (blocks.shape[0] * near)
    every = jnp.concatenate([ref[...] for ref in acts], axis=1)
    firsts = jnp.concatenate([ref[:, 0:pixels] for ref in acts], axis=1)
    if piece * videos > rows:
        blocks[:, :, piece - TILE:] = jnp.zeros((far, near, TILE, lanes), f32)

    for step in range(TAPS):
        right = jnp.concatenate(
            [windows(video, t + TAPS - 1 - step) for video in range(videos) for t in range(frames)], axis=0)
        result = dot(every, right, ROWS_COLS)

        def put(result, add, step=step):
            for place, (row, bank) in enumerate(slots):
                tile = result[:, place * lanes:(place + 1) * lanes]
                for k in range(min(per, TAPS - bank * per)):
                    tap = (step * TAPS + row) * TAPS + bank * per + k
                    done = 0
                    while done < chans:
                        index = tap * chans + done
                        owner, inside = index // rows, index % rows
                        part, at = inside // piece, inside % piece
                        length = min(chans - done, rows - inside, piece - at)
                        turn = (part - k) * cols % lanes
                        value = tile[done:done + length]
                        if turn:
                            value = pltpu.roll(value, turn, 1)
                        dest = blocks.at[owner // near, owner % near, at:at + length, part * cols:(part + 1) * cols]
                        value = value[:, part * cols:(part + 1) * cols]
                        dest[...] = dest[...] + value if add else value
                        done += length

        put(result, False)
        if step < TAPS - 1:
            @pl.when(device == 0)
            def _(step=step, put=put):
                right = jnp.concatenate([windows(video, 0) for video in range(videos)], axis=0)
                extra = dot(firsts, right, ROWS_COLS)
                for frame in range(1, TAPS - 1 - step):
                    right = jnp.concatenate([windows(video, frame) for video in range(videos)], axis=0)
                    extra = extra + dot(firsts, right, ROWS_COLS)
                put(extra, True)

    me = device % near
    own[...] = blocks[:, me]
    top, rest = halves(small_out[...])
    count = top.shape[0]
    lat_top, lat_rest = halves(lat_far[...])
    cells, depth = lat_top.shape
    for turn, send in enumerate(sends, 1):
        for k in range(far):
            send[k * piece:(k + 1) * piece] = blocks[k, paired(me, turn, near)].astype(bf16)
        at = far * piece
        send[at:at + count] = top
        send[at + count:at + 2 * count] = rest
        send[at + 2 * count:at + 2 * count + cells, :depth] = lat_top
        send[at + 2 * count + cells:at + 2 * count + 2 * cells, :depth] = lat_rest


def plane_sum_body(near, far, *refs):
    own, got, small, lat_own = refs[0], refs[1:near], refs[near], refs[near + 1]
    kept, sends, small_out, latent_grad, total = (
        refs[near + 2], refs[near + 3:near + far + 2], *refs[near + far + 2:])
    piece = own.shape[1]
    count = small.shape[0]
    cells, depth = lat_own.shape
    for k in range(far):
        total[k] = functools.reduce(lambda a, b: a + b[k * piece:(k + 1) * piece].astype(f32), got, own[k])
    at = far * piece

    def joined(ref, start, length):
        return ref[start:start + length].astype(f32) + ref[start + length:start + 2 * length].astype(f32)

    summed = functools.reduce(lambda a, b: a + joined(b, at, count), got, small[...])
    small_out[...] = summed
    latent_grad[...] = lat_own[...] + joined(got[0], at + 2 * count, cells)[:, :depth]
    me = lax.axis_index("ctx") // near
    kept[...] = total[me]
    top, rest = halves(summed)
    for turn, send in enumerate(sends, 1):
        send[0:piece] = total[paired(me, turn, far)].astype(bf16)
        send[piece:piece + count] = top
        send[piece + count:piece + 2 * count] = rest


def line_sum_body(far, *refs):
    kept, got, small, filter_grad, mod_grads, vector_grads = refs[0], refs[1:far], *refs[far:]
    piece, lanes = kept.shape
    count = small.shape[0]
    total = functools.reduce(lambda a, b: a + b[0:piece].astype(f32), got, kept[...])
    cols, rows = filter_grad.shape
    turned = total.T
    for part in range(lanes // cols):
        first, last = part * piece, min(rows, (part + 1) * piece)
        if first < last:
            filter_grad[:, first:last] = turned[part * cols:(part + 1) * cols, :last - first]
    summed = functools.reduce(
        lambda a, b: a + b[piece:piece + count].astype(f32) + b[piece + count:piece + 2 * count].astype(f32),
        got, small[...])
    split, length = mod_grads.shape[0], mod_grads.shape[0] + vector_grads.shape[0]
    for k in range(mod_grads.shape[1] // lanes):
        mod_grads[:, k * lanes:(k + 1) * lanes] = summed[k * length:k * length + split]
        vector_grads[:, k * lanes:(k + 1) * lanes] = summed[k * length + split:(k + 1) * length]


def local(features, grad_out, mean, rstd, latent, gamma, beta, ws, bs, wt, bt, kernel):
    _, frames, height, width, chans = features.shape
    outs = grad_out.shape[-1]
    depth, length = latent.shape[2:]
    count, videos = lax.axis_size("ctx"), lax.axis_size("vid")
    near = math.gcd(count, NEAR)
    far = count // near
    pixels = height * width
    size = frames * pixels
    rows, cols = TAPS**3 * chans // count, outs // videos
    piece = -(-rows // (TILE * videos)) * TILE
    gamma, beta, bs, bt = (value.reshape(1, chans) for value in (gamma, beta, bs, bt))
    feats = features.reshape(size, chans)
    grads = grad_out.reshape(size, outs)

    def along_ctx(value, target):
        return lax.ppermute(value, "ctx", [(s, target(s)) for s in range(count)])

    def others(value):
        return [value] + [
            lax.ppermute(value, "vid", [(s, (s + turn) % videos) for s in range(videos)])
            for turn in range(1, videos)]

    def near_got(values):
        return [along_ctx(value, lambda s: s - s % near + paired(s % near, turn, near))
                for turn, value in enumerate(values, 1)]

    def far_got(values):
        return [along_ctx(value, lambda s: paired(s // near, turn, far) * near + s % near)
                for turn, value in enumerate(values, 1)]

    beyond = lax.ppermute(grads, "ctx", [(s, s - 1) for s in range(1, count)])
    act_t, slope, normed, gain, tab = call(
        functools.partial(modulate_body, frames, height, width),
        (shaped((chans, size), bf16), shaped((size, chans)), shaped((size, chans)), shaped((pixels, chans)),
         shaped((length, chans))),
        name="modulate",
        far_args=tuple(range(10)),
    )(feats, mean, rstd, latent, gamma, beta, ws, bs, wt, bt)
    grads_all, acts_all, beyond_all = others(grads), others(act_t), others(beyond)
    small_rows = 2 * depth + 4
    cells = length // 2
    feats_grad, small, lat_own, lat_far = call(
        functools.partial(input_grad_body, frames, height, width),
        (shaped((size, chans), bf16), shaped((small_rows, chans)), shaped((cells, depth)), shaped((cells, depth))),
        (pltpu.VMEM((TAPS, 2 * frames, (height + 2) * width, outs), bf16), pltpu.VMEM((size, chans), f32)),
        name="input_grad",
        far_args=(0, 2, 7, 8, 9, 10, 11),
    )(grads, beyond, kernel, slope, normed, gain, tab, latent, ws, wt, gamma, beta)
    banks = -(-TAPS // min(videos, TAPS))
    count_small = -(-small_rows * (chans // outs) // TILE) * TILE
    extra = 2 * count_small + -(-2 * cells // TILE) * TILE
    own, *sends, small = call(
        functools.partial(filter_grad_body, frames, height, width, videos, near, piece),
        [shaped((far, piece, outs))] + [shaped((far * piece + extra, outs), bf16)] * (near - 1)
        + [shaped((count_small, outs))],
        (pltpu.VMEM((videos, banks, 2 * frames, (height + 2) * width, outs), bf16),
         pltpu.VMEM((far, near, piece, outs), f32)),
        name="filter_grad",
        far_args=(videos,),
    )(*acts_all, *grads_all, *beyond_all, *others(small), lat_far)
    kept, *sends, small, latent_grad = call(
        functools.partial(plane_sum_body, near, far),
        [shaped((piece, outs))] + [shaped((piece + 2 * count_small, outs), bf16)] * (far - 1)
        + [shaped((count_small, outs)), shaped((cells, depth))],
        (pltpu.VMEM((far, piece, outs), f32),),
        name="plane_sum",
    )(own, *near_got(sends), small, lat_own)
    filter_grad, mod_grads, vector_grads = call(
        functools.partial(line_sum_body, far),
        (shaped((cols, rows)), shaped((2 * depth, chans)), shaped((4, chans))),
        name="line_sum",
    )(kept, *far_got(sends), small)
    return (
        feats_grad.reshape(features.shape),
        filter_grad.T,
        mod_grads.reshape(2, depth, chans),
        vector_grads,
        latent_grad.T[None, None],
    )


def solution(mesh):
    split = P("vid", "ctx", None, None, None)
    return jax.shard_map(
        local,
        mesh=mesh,
        in_specs=(split, split, P("vid", None), P("vid", None), P("vid", None, None, None)) + (P(),) * 7,
        out_specs=(split, P("ctx", "vid"), P(), P(), P("vid", "ctx", None, None)),
        check_vma=False,
    )
```

profile of v0, /device:TPU:0, one launch (start us, length us, event | category | flops | bytes accessed | tf_op | source)
XLA Modules:
  0.0 49.0 jit_solution(2275582234745755418)
XLA Ops:
  0.6 1.3 %collective-permute-start = (bf16[512,128]{1,0:T(8,128)(2,1)}, bf16[512,128]{1,0:T(8,128)(2,1)S(1)}, u32[]{:S(2)}, u32[]{:S(2)}) collective-permute-start(bf16[512,128]{1,0:T(8,128)(2,1)} %bitcast.12), channel_id=1, source_target_pairs={{2,0},{4,2},{6,4},{8,6},{10,8},{12,10},{14,12},{16,14},{18,16},{20... | collective-permute-start | bytes 393224 | tf_op jit(solution)/shard_map/ppermute | solution.py:364
  1.9 2.1 %modulate.1 = (bf16[256,512]{1,0:T(8,128)(2,1)S(1)}, f32[512,256]{1,0:T(8,128)S(1)}, f32[512,256]{1,0:T(8,128)S(1)}, f32[256,256]{1,0:T(8,128)S(1)}, f32[16,256]{1,0:T(8,128)S(1)}) custom-call(bf16[512,256]{1,0:T(8,128)(2,1)} %bitcast.16, f32[1,32]{1,0:T(1,128)} %refs_1_.1, f32[1,32]{1,0:T(1,128)} %refs_2_.2, f32[1,8,16,16]{3,2,1,0:T(8,128)} %refs_7_.1, ...), custom_call_target="tpu_custom_call" | custom-call | tf_op jit(solution)/shard_map/modulate/pallas_call | solution.py:44
  4.0 0.5 %collective-permute-start.1 = (bf16[256,512]{1,0:T(8,128)(2,1)S(1)}, bf16[256,512]{1,0:T(8,128)(2,1)S(1)}, u32[]{:S(2)}, u32[]{:S(2)}) collective-permute-start(bf16[256,512]{1,0:T(8,128)(2,1)S(1)} %get-tuple-element.33.refs_0_), channel_id=1, source_target_pairs={{0,1},{1,0},{2,3},{3,2},{4,5},{5,4},{6,7},{7,6},{8,9},{9,8},{10,11... | collective-permute-start | bytes 786440 | tf_op jit(solution)/shard_map/ppermute | solution.py:353
  4.6 0.1 collective-permute-start.2
  4.6 4.5 %collective-permute-done.refs_1_.refs_4_ = bf16[512,128]{1,0:T(8,128)(2,1)S(1)} collective-permute-done((bf16[512,128]{1,0:T(8,128)(2,1)}, bf16[512,128]{1,0:T(8,128)(2,1)S(1)}, u32[]{:S(2)}, u32[]{:S(2)}) %collective-permute-start) | collective-permute-done | bytes 131104 | tf_op jit(solution)/shard_map/ppermute | solution.py:364
  9.2 0.0 collective-permute-start.3
  9.2 4.6 %input_grad.1 = (bf16[512,256]{1,0:T(8,128)(2,1)}, f32[36,256]{1,0:T(8,128)S(1)}, f32[8,16]{1,0:T(8,128)S(1)}, f32[8,16]{1,0:T(8,128)S(1)}) custom-call(bf16[512,128]{1,0:T(8,128)(2,1)} %bitcast.14, bf16[512,128]{1,0:T(8,128)(2,1)S(1)} %collective-permute-done.refs_1_.refs_4_, bf16[6912,128]{1,0:T(8,128)(2,1)} %refs_2_.3, ...), custom_call_target="tpu_custom_call" | custom-call | tf_op jit(solution)/shard_map/input_grad/pallas_call | solution.py:44
  13.8 0.6 %collective-permute-start.4 = (f32[36,256]{1,0:T(8,128)S(1)}, f32[36,256]{1,0:T(8,128)S(1)}, u32[]{:S(2)}, u32[]{:S(2)}) collective-permute-start(f32[36,256]{1,0:T(8,128)S(1)} %get-tuple-element.34.refs_6_), channel_id=1, source_target_pairs={{0,1},{1,0},{2,3},{3,2},{4,5},{5,4},{6,7},{7,6},{8,9},{9,8},{10,11... | collective-permute-start | bytes 110600 | tf_op jit(solution)/shard_map/ppermute | solution.py:353
  14.3 0.0 collective-permute-done.2.refs_3_
  14.3 0.9 %collective-permute-done.4.refs_7_ = f32[36,256]{1,0:T(8,128)S(1)} collective-permute-done((f32[36,256]{1,0:T(8,128)S(1)}, f32[36,256]{1,0:T(8,128)S(1)}, u32[]{:S(2)}, u32[]{:S(2)}) %collective-permute-start.4) | collective-permute-done | bytes 36896 | tf_op jit(solution)/shard_map/ppermute | solution.py:353
  15.2 0.0 collective-permute-done.3.refs_5_
  15.2 0.0 collective-permute-done.1.refs_1_
  15.2 4.6 %filter_grad.1 = (f32[4,224,128]{2,1,0:T(8,128)S(1)}, bf16[1072,128]{1,0:T(8,128)(2,1)S(1)}, bf16[1072,128]{1,0:T(8,128)(2,1)S(1)}, bf16[1072,128]{1,0:T(8,128)(2,1)S(1)}, f32[80,128]{1,0:T(8,128)S(1)}) custom-call(bf16[256,512]{1,0:T(8,128)(2,1)S(1)} %get-tuple-element.33.refs_0_, bf16[256,512]{1,0:T(8,128)(2,1)S(1)} %collective-permute-done.1.refs_1_, ...), custom_call_target="tpu_custom_call" | custom-call | tf_op jit(solution)/shard_map/filter_grad/pallas_call | solution.py:44
  19.8 0.9 %collective-permute-start.5 = (bf16[1072,128]{1,0:T(8,128)(2,1)S(1)}, bf16[1072,128]{1,0:T(8,128)(2,1)S(1)}, u32[]{:S(2)}, u32[]{:S(2)}) collective-permute-start(bf16[1072,128]{1,0:T(8,128)(2,1)S(1)} %get-tuple-element.37), channel_id=1, source_target_pairs={{0,2},{2,0},{4,6},{6,4},{8,10},{10,8},{12,14},{14,12},{16,18},{18,... | collective-permute-start | bytes 823304 | tf_op jit(solution)/shard_map/ppermute | solution.py:349
  20.6 2.4 %collective-permute-start.6 = (bf16[1072,128]{1,0:T(8,128)(2,1)S(1)}, bf16[1072,128]{1,0:T(8,128)(2,1)S(1)}, u32[]{:S(2)}, u32[]{:S(2)}) collective-permute-start(bf16[1072,128]{1,0:T(8,128)(2,1)S(1)} %get-tuple-element.38), channel_id=1, source_target_pairs={{0,4},{2,6},{4,0},{6,2},{8,12},{10,14},{12,8},{14,10},{16,20},{18,... | collective-permute-start | bytes 823304 | tf_op jit(solution)/shard_map/ppermute | solution.py:349
  23.1 0.3 collective-permute-start.7
  23.3 5.9 %collective-permute-done.5.refs_1_ = bf16[1072,128]{1,0:T(8,128)(2,1)S(1)} collective-permute-done((bf16[1072,128]{1,0:T(8,128)(2,1)S(1)}, bf16[1072,128]{1,0:T(8,128)(2,1)S(1)}, u32[]{:S(2)}, u32[]{:S(2)}) %collective-permute-start.5) | collective-permute-done | bytes 274464 | tf_op jit(solution)/shard_map/ppermute | solution.py:349
  29.2 6.5 %collective-permute-done.6.refs_2_ = bf16[1072,128]{1,0:T(8,128)(2,1)S(1)} collective-permute-done((bf16[1072,128]{1,0:T(8,128)(2,1)S(1)}, bf16[1072,128]{1,0:T(8,128)(2,1)S(1)}, u32[]{:S(2)}, u32[]{:S(2)}) %collective-permute-start.6) | collective-permute-done | bytes 274464 | tf_op jit(solution)/shard_map/ppermute | solution.py:349
  35.8 0.0 collective-permute-done.7.refs_3_
  35.8 0.7 %plane_sum.1 = (f32[224,128]{1,0:T(8,128)S(1)}, bf16[384,128]{1,0:T(8,128)(2,1)S(1)}, bf16[384,128]{1,0:T(8,128)(2,1)S(1)}, bf16[384,128]{1,0:T(8,128)(2,1)S(1)}...) custom-call(f32[4,224,128]{2,1,0:T(8,128)S(1)} %get-tuple-element.36.refs_0_, ...), custom_call_target="tpu_custom_call" | custom-call | tf_op jit(solution)/shard_map/plane_sum/pallas_call | solution.py:44
  36.5 1.6 %collective-permute-start.8 = (bf16[384,128]{1,0:T(8,128)(2,1)S(1)}, bf16[384,128]{1,0:T(8,128)(2,1)S(1)}, u32[]{:S(2)}, u32[]{:S(2)}) collective-permute-start(bf16[384,128]{1,0:T(8,128)(2,1)S(1)} %get-tuple-element.43), channel_id=1, source_target_pairs={{0,8},{2,10},{4,12},{6,14},{8,0},{10,2},{12,4},{14,6},{16,24},{18,... | collective-permute-start | bytes 294920 | tf_op jit(solution)/shard_map/ppermute | solution.py:349
  38.1 1.9 %collective-permute-start.9 = (bf16[384,128]{1,0:T(8,128)(2,1)S(1)}, bf16[384,128]{1,0:T(8,128)(2,1)S(1)}, u32[]{:S(2)}, u32[]{:S(2)}) collective-permute-start(bf16[384,128]{1,0:T(8,128)(2,1)S(1)} %get-tuple-element.44), channel_id=1, source_target_pairs={{0,16},{2,18},{4,20},{6,22},{8,24},{10,26},{12,28},{14,30},{16,0},... | collective-permute-start | bytes 294920 | tf_op jit(solution)/shard_map/ppermute | solution.py:349
  40.0 0.9 %collective-permute-start.10 = (bf16[384,128]{1,0:T(8,128)(2,1)S(1)}, bf16[384,128]{1,0:T(8,128)(2,1)S(1)}, u32[]{:S(2)}, u32[]{:S(2)}) collective-permute-start(bf16[384,128]{1,0:T(8,128)(2,1)S(1)} %get-tuple-element.45), channel_id=1, source_target_pairs={{0,24},{2,26},{4,28},{6,30},{8,16},{10,18},{12,20},{14,22},{16,8},... | collective-permute-start | bytes 294920 | tf_op jit(solution)/shard_map/ppermute | solution.py:349
  40.9 1.2 %collective-permute-done.8.refs_1_ = bf16[384,128]{1,0:T(8,128)(2,1)S(1)} collective-permute-done((bf16[384,128]{1,0:T(8,128)(2,1)S(1)}, bf16[384,128]{1,0:T(8,128)(2,1)S(1)}, u32[]{:S(2)}, u32[]{:S(2)}) %collective-permute-start.8) | collective-permute-done | bytes 98336 | tf_op jit(solution)/shard_map/ppermute | solution.py:349
  42.1 6.1 %collective-permute-done.9.refs_2_ = bf16[384,128]{1,0:T(8,128)(2,1)S(1)} collective-permute-done((bf16[384,128]{1,0:T(8,128)(2,1)S(1)}, bf16[384,128]{1,0:T(8,128)(2,1)S(1)}, u32[]{:S(2)}, u32[]{:S(2)}) %collective-permute-start.9) | collective-permute-done | bytes 98336 | tf_op jit(solution)/shard_map/ppermute | solution.py:349
  48.2 0.0 collective-permute-done.10.refs_3_
  48.2 0.8 %line_sum.1 = (f32[64,432]{1,0:T(8,128)}, f32[32,256]{1,0:T(8,128)}, f32[4,256]{1,0:T(4,128)}) custom-call(f32[224,128]{1,0:T(8,128)S(1)} %get-tuple-element.42.refs_0_, bf16[384,128]{1,0:T(8,128)(2,1)S(1)} %collective-permute-done.8.refs_1_, bf16[384,128]{1,0:T(8,128)(2,1)S(1)} %collective-permute-done.9.refs_2_, ...), custom_call_target="tpu_custom_call" | custom-call | tf_op jit(solution)/shard_map/line_sum/pallas_call | solution.py:44
Async XLA Ops:
  0.6 8.5 %collective-permute-start = (bf16[512,128]{1,0:T(8,128)(2,1)}, bf16[512,128]{1,0:T(8,128)(2,1)S(1)}, u32[]{:S(2)}, u32[]{:S(2)}) collective-permute-start(bf16[512,128]{1,0:T(8,128)(2,1)} %bitcast.12), channel_id=1, source_target_pairs={{2,0},{4,2},{6,4},{8,6},{10,8},{12,10},{14,12},{16,14},{18,16},{20... | collective-permute-start | bytes 393224 | tf_op jit(solution)/shard_map/ppermute | solution.py:364
  4.0 11.2 %collective-permute-start.1 = (bf16[256,512]{1,0:T(8,128)(2,1)S(1)}, bf16[256,512]{1,0:T(8,128)(2,1)S(1)}, u32[]{:S(2)}, u32[]{:S(2)}) collective-permute-start(bf16[256,512]{1,0:T(8,128)(2,1)S(1)} %get-tuple-element.33.refs_0_), channel_id=1, source_target_pairs={{0,1},{1,0},{2,3},{3,2},{4,5},{5,4},{6,7},{7,6},{8,9},{9,8},{10,11... | collective-permute-start | bytes 786440 | tf_op jit(solution)/shard_map/ppermute | solution.py:353
  4.6 9.8 %collective-permute-start.2 = (bf16[512,128]{1,0:T(8,128)(2,1)}, bf16[512,128]{1,0:T(8,128)(2,1)S(1)}, u32[]{:S(2)}, u32[]{:S(2)}) collective-permute-start(bf16[512,128]{1,0:T(8,128)(2,1)} %bitcast.13), channel_id=1, source_target_pairs={{0,1},{1,0},{2,3},{3,2},{4,5},{5,4},{6,7},{7,6},{8,9},{9,8},{10,11... | collective-permute-start | bytes 393224 | tf_op jit(solution)/shard_map/ppermute | solution.py:353
  9.2 6.0 %collective-permute-start.3 = (bf16[512,128]{1,0:T(8,128)(2,1)S(1)}, bf16[512,128]{1,0:T(8,128)(2,1)S(1)}, u32[]{:S(2)}, u32[]{:S(2)}) collective-permute-start(bf16[512,128]{1,0:T(8,128)(2,1)S(1)} %collective-permute-done.refs_1_.refs_4_), channel_id=1, source_target_pairs={{0,1},{1,0},{2,3},{3,2},{4,5},{5,4},{6,7},{7,6},{8,9},{9,8},{10,11... | collective-permute-start | bytes 393224 | tf_op jit(solution)/shard_map/ppermute | solution.py:353
  13.8 1.4 %collective-permute-start.4 = (f32[36,256]{1,0:T(8,128)S(1)}, f32[36,256]{1,0:T(8,128)S(1)}, u32[]{:S(2)}, u32[]{:S(2)}) collective-permute-start(f32[36,256]{1,0:T(8,128)S(1)} %get-tuple-element.34.refs_6_), channel_id=1, source_target_pairs={{0,1},{1,0},{2,3},{3,2},{4,5},{5,4},{6,7},{7,6},{8,9},{9,8},{10,11... | collective-permute-start | bytes 110600 | tf_op jit(solution)/shard_map/ppermute | solution.py:353
  19.8 9.5 %collective-permute-start.5 = (bf16[1072,128]{1,0:T(8,128)(2,1)S(1)}, bf16[1072,128]{1,0:T(8,128)(2,1)S(1)}, u32[]{:S(2)}, u32[]{:S(2)}) collective-permute-start(bf16[1072,128]{1,0:T(8,128)(2,1)S(1)} %get-tuple-element.37), channel_id=1, source_target_pairs={{0,2},{2,0},{4,6},{6,4},{8,10},{10,8},{12,14},{14,12},{16,18},{18,... | collective-permute-start | bytes 823304 | tf_op jit(solution)/shard_map/ppermute | solution.py:349
  20.6 15.1 %collective-permute-start.6 = (bf16[1072,128]{1,0:T(8,128)(2,1)S(1)}, bf16[1072,128]{1,0:T(8,128)(2,1)S(1)}, u32[]{:S(2)}, u32[]{:S(2)}) collective-permute-start(bf16[1072,128]{1,0:T(8,128)(2,1)S(1)} %get-tuple-element.38), channel_id=1, source_target_pairs={{0,4},{2,6},{4,0},{6,2},{8,12},{10,14},{12,8},{14,10},{16,20},{18,... | collective-permute-start | bytes 823304 | tf_op jit(solution)/shard_map/ppermute | solution.py:349
  23.1 12.7 %collective-permute-start.7 = (bf16[1072,128]{1,0:T(8,128)(2,1)S(1)}, bf16[1072,128]{1,0:T(8,128)(2,1)S(1)}, u32[]{:S(2)}, u32[]{:S(2)}) collective-permute-start(bf16[1072,128]{1,0:T(8,128)(2,1)S(1)} %get-tuple-element.39), channel_id=1, source_target_pairs={{0,6},{2,4},{4,2},{6,0},{8,14},{10,12},{12,10},{14,8},{16,22},{18,... | collective-permute-start | bytes 823304 | tf_op jit(solution)/shard_map/ppermute | solution.py:349
  36.5 5.6 %collective-permute-start.8 = (bf16[384,128]{1,0:T(8,128)(2,1)S(1)}, bf16[384,128]{1,0:T(8,128)(2,1)S(1)}, u32[]{:S(2)}, u32[]{:S(2)}) collective-permute-start(bf16[384,128]{1,0:T(8,128)(2,1)S(1)} %get-tuple-element.43), channel_id=1, source_target_pairs={{0,8},{2,10},{4,12},{6,14},{8,0},{10,2},{12,4},{14,6},{16,24},{18,... | collective-permute-start | bytes 294920 | tf_op jit(solution)/shard_map/ppermute | solution.py:349
  38.1 10.1 %collective-permute-start.9 = (bf16[384,128]{1,0:T(8,128)(2,1)S(1)}, bf16[384,128]{1,0:T(8,128)(2,1)S(1)}, u32[]{:S(2)}, u32[]{:S(2)}) collective-permute-start(bf16[384,128]{1,0:T(8,128)(2,1)S(1)} %get-tuple-element.44), channel_id=1, source_target_pairs={{0,16},{2,18},{4,20},{6,22},{8,24},{10,26},{12,28},{14,30},{16,0},... | collective-permute-start | bytes 294920 | tf_op jit(solution)/shard_map/ppermute | solution.py:349
  40.0 8.2 %collective-permute-start.10 = (bf16[384,128]{1,0:T(8,128)(2,1)S(1)}, bf16[384,128]{1,0:T(8,128)(2,1)S(1)}, u32[]{:S(2)}, u32[]{:S(2)}) collective-permute-start(bf16[384,128]{1,0:T(8,128)(2,1)S(1)} %get-tuple-element.45), channel_id=1, source_target_pairs={{0,24},{2,26},{4,28},{6,30},{8,16},{10,18},{12,20},{14,22},{16,8},... | collective-permute-start | bytes 294920 | tf_op jit(solution)/shard_map/ppermute | solution.py:349
where the time goes:
time: 49.2 us; the launch traced here: 49 us
  waiting for transfers between devices  25.2 us (51%)
  Pallas kernels  12.8 us (26%)
  starting transfers between devices  10.4 us (21%)
  between operations  0.68 us (1%)
    ppermute x6, waiting for transfers between devices, along_ctx(): return lax.ppermute(value, 'ctx', [(s, target(s)) for s in range(count)])  19.7 us
    pallas_call x5, Pallas kernels, run(): pl.pallas_call(full if far_args else body, out_shape=outs, in_specs=[pl.B...  12.8 us
    ppermute x6, starting transfers between devices, along_ctx(): return lax.ppermute(value, 'ctx', [(s, target(s)) for s in range(count)])  7.94 us
    ppermute x1, waiting for transfers between devices, local(): beyond = lax.ppermute(grads, 'ctx', [(s, s - 1) for s in range(1, count)])  4.55 us
    ppermute x1, starting transfers between devices, local(): beyond = lax.ppermute(grads, 'ctx', [(s, s - 1) for s in range(1, count)])  1.29 us
    ppermute x4, starting transfers between devices, others(): lax.ppermute(value, 'vid', [(s, (s + turn) % videos) for s in range(video...  1.15 us
  transfers between devices with their start and end apart: 11, of which 6 were waited for; matrix products, arithmetic and copies ran while one was open for 0% of the time, Pallas kernels for 14%

commit v1 on v0

--- a/solution.py
+++ b/solution.py
@@ -188,7 +188,7 @@
     beyond, refs = refs[:videos], refs[videos:]
     smalls, refs = refs[:videos], refs[videos:]
     lat_far, own, refs = refs[0], refs[1], refs[2:]
-    sends, small_out, packs, blocks = refs[:near - 1], refs[near - 1], refs[near], refs[near + 1]
+    sends, small_out, packs, blocks = refs
     pixels = height * width
     chans = acts[0].shape[0]
     lanes = grads[0].shape[1]
@@ -274,7 +274,8 @@
     count = top.shape[0]
     lat_top, lat_rest = halves(lat_far[...])
     cells, depth = lat_top.shape
-    for turn, send in enumerate(sends, 1):
+    for turn in range(1, near):
+        send = sends.at[paired(me, turn, near)]
         for k in range(far):
             send[k * piece:(k + 1) * piece] = blocks[k, paired(me, turn, near)].astype(bf16)
         at = far * piece
@@ -285,9 +286,9 @@
 
 
 def plane_sum_body(near, far, *refs):
-    own, got, small, lat_own = refs[0], refs[1:near], refs[near], refs[near + 1]
-    kept, sends, small_out, latent_grad, total = (
-        refs[near + 2], refs[near + 3:near + far + 2], *refs[near + far + 2:])
+    own, got_all, small, lat_own, kept, sends, small_out, latent_grad, total = refs
+    place = lax.axis_index("ctx") % near
+    got = [got_all.at[paired(place, turn, near)] for turn in range(1, near)]
     piece = own.shape[1]
     count = small.shape[0]
     cells, depth = lat_own.shape
@@ -304,14 +305,17 @@
     me = lax.axis_index("ctx") // near
     kept[...] = total[me]
     top, rest = halves(summed)
-    for turn, send in enumerate(sends, 1):
+    for turn in range(1, far):
+        send = sends.at[paired(me, turn, far)]
         send[0:piece] = total[paired(me, turn, far)].astype(bf16)
         send[piece:piece + count] = top
         send[piece + count:piece + 2 * count] = rest
 
 
 def line_sum_body(far, *refs):
-    kept, got, small, filter_grad, mod_grads, vector_grads = refs[0], refs[1:far], *refs[far:]
+    kept, got_all, small, filter_grad, mod_grads, vector_grads = refs
+    place = lax.axis_index("ctx") // (lax.axis_size("ctx") // far)
+    got = [got_all.at[paired(place, turn, far)] for turn in range(1, far)]
     piece, lanes = kept.shape
     count = small.shape[0]
     total = functools.reduce(lambda a, b: a + b[0:piece].astype(f32), got, kept[...])
@@ -345,21 +349,18 @@
     feats = features.reshape(size, chans)
     grads = grad_out.reshape(size, outs)
 
-    def along_ctx(value, target):
-        return lax.ppermute(value, "ctx", [(s, target(s)) for s in range(count)])
-
     def others(value):
         return [value] + [
             lax.ppermute(value, "vid", [(s, (s + turn) % videos) for s in range(videos)])
             for turn in range(1, videos)]
 
     def near_got(values):
-        return [along_ctx(value, lambda s: s - s % near + paired(s % near, turn, near))
-                for turn, value in enumerate(values, 1)]
+        groups = [[line * near + k for k in range(near)] for line in range(far)]
+        return lax.all_to_all(values, "ctx", 0, 0, axis_index_groups=groups)
 
     def far_got(values):
-        return [along_ctx(value, lambda s: paired(s // near, turn, far) * near + s % near)
-                for turn, value in enumerate(values, 1)]
+        groups = [[k * near + place for k in range(far)] for place in range(near)]
+        return lax.all_to_all(values, "ctx", 0, 0, axis_index_groups=groups)
 
     beyond = lax.ppermute(grads, "ctx", [(s, s - 1) for s in range(1, count)])
     act_t, slope, normed, gain, tab = call(
@@ -382,27 +383,27 @@
     banks = -(-TAPS // min(videos, TAPS))
     count_small = -(-small_rows * (chans // outs) // TILE) * TILE
     extra = 2 * count_small + -(-2 * cells // TILE) * TILE
-    own, *sends, small = call(
+    own, sends, small = call(
         functools.partial(filter_grad_body, frames, height, width, videos, near, piece),
-        [shaped((far, piece, outs))] + [shaped((far * piece + extra, outs), bf16)] * (near - 1)
+        [shaped((far, piece, outs))] + [shaped((near, far * piece + extra, outs), bf16)]
         + [shaped((count_small, outs))],
         (pltpu.VMEM((videos, banks, 2 * frames, (height + 2) * width, outs), bf16),
          pltpu.VMEM((far, near, piece, outs), f32)),
         name="filter_grad",
         far_args=(videos,),
     )(*acts_all, *grads_all, *beyond_all, *others(small), lat_far)
-    kept, *sends, small, latent_grad = call(
+    kept, sends, small, latent_grad = call(
         functools.partial(plane_sum_body, near, far),
-        [shaped((piece, outs))] + [shaped((piece + 2 * count_small, outs), bf16)] * (far - 1)
+        [shaped((piece, outs))] + [shaped((far, piece + 2 * count_small, outs), bf16)]
         + [shaped((count_small, outs)), shaped((cells, depth))],
         (pltpu.VMEM((far, piece, outs), f32),),
         name="plane_sum",
-    )(own, *near_got(sends), small, lat_own)
+    )(own, near_got(sends), small, lat_own)
     filter_grad, mod_grads, vector_grads = call(
         functools.partial(line_sum_body, far),
         (shaped((cols, rows)), shaped((2 * depth, chans)), shaped((4, chans))),
         name="line_sum",
-    )(kept, *far_got(sends), small)
+    )(kept, far_got(sends), small)
     return (
         feats_grad.reshape(features.shape),
         filter_grad.T,

time: 49.2 us -> 55 us (1.12)
  blocking collectives: 0 us -> 33.4 us
  waiting for transfers between devices: 25.2 us -> 5.42 us
  starting transfers between devices: 10.4 us -> 2.44 us
    all_to_all x0 -> x2, blocking collectives: none -> 33.4 us  [the longest x1 19.1 us: near_got(): return lax.all_to_all(values, 'ctx', 0, 0, axis_index_groups=groups)]
    ppermute x6 -> x0, waiting for transfers between devices: 19.7 us -> none  [along_ctx(): return lax.ppermute(value, 'ctx', [(s, target(s)) for s in range(count)])]
    ppermute x6 -> x0, starting transfers between devices: 7.94 us -> none  [along_ctx(): return lax.ppermute(value, 'ctx', [(s, target(s)) for s in range(count)])]
  transfers between devices with their start and end apart: 11 -> 5, of which waited for: 6 -> 2; matrix products, arithmetic and copies ran while one was open for 0% -> 0% of each run, Pallas kernels for 14% -> 12%
where the time goes in v1:
time: 55 us; the launch traced here: 54.8 us
  blocking collectives  33.4 us (61%)
  Pallas kernels  12.8 us (23%)
  waiting for transfers between devices  5.42 us (10%)
  starting transfers between devices  2.44 us (4%)
  between operations  0.67 us (1%)
    all_to_all x1, blocking collectives, near_got(): return lax.all_to_all(values, 'ctx', 0, 0, axis_index_groups=groups)  19.1 us
    all_to_all x1, blocking collectives, far_got(): return lax.all_to_all(values, 'ctx', 0, 0, axis_index_groups=groups)  14.3 us
    pallas_call x5, Pallas kernels, run(): pl.pallas_call(full if far_args else body, out_shape=outs, in_specs=[pl.B...  12.8 us
    ppermute x1, waiting for transfers between devices, local(): beyond = lax.ppermute(grads, 'ctx', [(s, s - 1) for s in range(1, count)])  4.55 us
    ppermute x1, starting transfers between devices, local(): beyond = lax.ppermute(grads, 'ctx', [(s, s - 1) for s in range(1, count)])  1.29 us
    ppermute x4, starting transfers between devices, others(): lax.ppermute(value, 'vid', [(s, (s + turn) % videos) for s in range(video...  1.15 us
  transfers between devices with their start and end apart: 5, of which 2 were waited for; matrix products, arithmetic and copies ran while one was open for 0% of the time, Pallas kernels for 12%

profile of v1, /device:TPU:0, one launch (start us, length us, event | category | flops | bytes accessed | tf_op | source)
XLA Modules:
  0.0 54.8 jit_solution(771831712534476473)
XLA Ops:
  0.6 1.3 %collective-permute-start = (bf16[512,128]{1,0:T(8,128)(2,1)}, bf16[512,128]{1,0:T(8,128)(2,1)S(1)}, u32[]{:S(2)}, u32[]{:S(2)}) collective-permute-start(bf16[512,128]{1,0:T(8,128)(2,1)} %bitcast.12), channel_id=1, source_target_pairs={{2,0},{4,2},{6,4},{8,6},{10,8},{12,10},{14,12},{16,14},{18,16},{20... | collective-permute-start | bytes 393224 | tf_op jit(solution)/shard_map/ppermute | solution.py:365
  1.9 2.1 %modulate.1 = (bf16[256,512]{1,0:T(8,128)(2,1)S(1)}, f32[512,256]{1,0:T(8,128)S(1)}, f32[512,256]{1,0:T(8,128)S(1)}, f32[256,256]{1,0:T(8,128)S(1)}, f32[16,256]{1,0:T(8,128)S(1)}) custom-call(bf16[512,256]{1,0:T(8,128)(2,1)} %bitcast.16, f32[1,32]{1,0:T(1,128)} %refs_1_.1, f32[1,32]{1,0:T(1,128)} %refs_2_.2, f32[1,8,16,16]{3,2,1,0:T(8,128)} %refs_7_.1, ...), custom_call_target="tpu_custom_call" | custom-call | tf_op jit(solution)/shard_map/modulate/pallas_call | solution.py:44
  4.0 0.5 collective-permute-start.1
  4.6 0.1 collective-permute-start.2
  4.6 4.5 %collective-permute-done.refs_1_.refs_4_ = bf16[512,128]{1,0:T(8,128)(2,1)S(1)} collective-permute-done((bf16[512,128]{1,0:T(8,128)(2,1)}, bf16[512,128]{1,0:T(8,128)(2,1)S(1)}, u32[]{:S(2)}, u32[]{:S(2)}) %collective-permute-start) | collective-permute-done | bytes 131104 | tf_op jit(solution)/shard_map/ppermute | solution.py:365
  9.2 0.0 collective-permute-start.3
  9.2 4.6 %input_grad.1 = (bf16[512,256]{1,0:T(8,128)(2,1)}, f32[36,256]{1,0:T(8,128)S(1)}, f32[8,16]{1,0:T(8,128)S(1)}, f32[8,16]{1,0:T(8,128)S(1)}) custom-call(bf16[512,128]{1,0:T(8,128)(2,1)} %bitcast.14, bf16[512,128]{1,0:T(8,128)(2,1)S(1)} %collective-permute-done.refs_1_.refs_4_, bf16[6912,128]{1,0:T(8,128)(2,1)} %refs_2_.3, ...), custom_call_target="tpu_custom_call" | custom-call | tf_op jit(solution)/shard_map/input_grad/pallas_call | solution.py:44
  13.8 0.6 %collective-permute-start.4 = (f32[36,256]{1,0:T(8,128)S(1)}, f32[36,256]{1,0:T(8,128)S(1)}, u32[]{:S(2)}, u32[]{:S(2)}) collective-permute-start(f32[36,256]{1,0:T(8,128)S(1)} %get-tuple-element.30.refs_6_), channel_id=1, source_target_pairs={{0,1},{1,0},{2,3},{3,2},{4,5},{5,4},{6,7},{7,6},{8,9},{9,8},{10,11... | collective-permute-start | bytes 110600 | tf_op jit(solution)/shard_map/ppermute | solution.py:354
  14.3 0.0 collective-permute-done.2.refs_3_
  14.3 0.9 %collective-permute-done.4.refs_7_ = f32[36,256]{1,0:T(8,128)S(1)} collective-permute-done((f32[36,256]{1,0:T(8,128)S(1)}, f32[36,256]{1,0:T(8,128)S(1)}, u32[]{:S(2)}, u32[]{:S(2)}) %collective-permute-start.4) | collective-permute-done | bytes 36896 | tf_op jit(solution)/shard_map/ppermute | solution.py:354
  15.2 0.0 collective-permute-done.3.refs_5_
  15.2 0.0 collective-permute-done.1.refs_1_
  15.2 4.5 %filter_grad.1 = (f32[4,224,128]{2,1,0:T(8,128)S(1)}, bf16[4,1072,128]{2,1,0:T(8,128)(2,1)S(1)}, f32[80,128]{1,0:T(8,128)S(1)}) custom-call(bf16[256,512]{1,0:T(8,128)(2,1)S(1)} %get-tuple-element.29.refs_0_, bf16[256,512]{1,0:T(8,128)(2,1)S(1)} %collective-permute-done.1.refs_1_, bf16[512,128]{1,0:T(8,128)(2,1)} %bitcast.15, ...), custom_call_target="tpu_custom_call" | custom-call | tf_op jit(solution)/shard_map/filter_grad/pallas_call | solution.py:44
  19.8 19.1 %all_to_all.10.refs_1_ = bf16[4,1072,128]{2,1,0:T(8,128)(2,1)S(1)} all-to-all(bf16[4,1072,128]{2,1,0:T(8,128)(2,1)S(1)} %get-tuple-element.33), channel_id=1, replica_groups={{0,2,4,6},{8,10,12,14},{16,18,20,22},{24,26,28,30},{1,3,5,7},{9,11,13,1..., dimensions={0} | all-to-all | bytes 2195456 | tf_op jit(solution)/shard_map/all_to_all | solution.py:359
  38.9 0.7 %plane_sum.1 = (f32[224,128]{1,0:T(8,128)S(1)}, bf16[4,384,128]{2,1,0:T(8,128)(2,1)S(1)}, f32[80,128]{1,0:T(8,128)S(1)}, f32[8,16]{1,0:T(8,128)}) custom-call(f32[4,224,128]{2,1,0:T(8,128)S(1)} %get-tuple-element.32.refs_0_, bf16[4,1072,128]{2,1,0:T(8,128)(2,1)S(1)} %all_to_all.10.refs_1_, f32[80,128]{1,0:T(8,128)S(1)} %get-tuple-element.34.refs_2_, ...), custom_call_target="tpu_custom_call" | custom-call | tf_op jit(solution)/shard_map/plane_sum/pallas_call | solution.py:44
  39.6 14.3 %all_to_all.11.refs_1_ = bf16[4,384,128]{2,1,0:T(8,128)(2,1)S(1)} all-to-all(bf16[4,384,128]{2,1,0:T(8,128)(2,1)S(1)} %get-tuple-element.37), channel_id=1, replica_groups={{0,8,16,24},{2,10,18,26},{4,12,20,28},{6,14,22,30},{1,9,17,25},{3,11,19..., dimensions={0} | all-to-all | bytes 786432 | tf_op jit(solution)/shard_map/all_to_all | solution.py:363
  53.9 0.8 %line_sum.1 = (f32[64,432]{1,0:T(8,128)}, f32[32,256]{1,0:T(8,128)}, f32[4,256]{1,0:T(4,128)}) custom-call(f32[224,128]{1,0:T(8,128)S(1)} %get-tuple-element.36.refs_0_, bf16[4,384,128]{2,1,0:T(8,128)(2,1)S(1)} %all_to_all.11.refs_1_, f32[80,128]{1,0:T(8,128)S(1)} %get-tuple-element.38.refs_2_), custom_call_target="tpu_custom_call" | custom-call | tf_op jit(solution)/shard_map/line_sum/pallas_call | solution.py:44
Async XLA Ops:
  0.6 8.5 %collective-permute-start = (bf16[512,128]{1,0:T(8,128)(2,1)}, bf16[512,128]{1,0:T(8,128)(2,1)S(1)}, u32[]{:S(2)}, u32[]{:S(2)}) collective-permute-start(bf16[512,128]{1,0:T(8,128)(2,1)} %bitcast.12), channel_id=1, source_target_pairs={{2,0},{4,2},{6,4},{8,6},{10,8},{12,10},{14,12},{16,14},{18,16},{20... | collective-permute-start | bytes 393224 | tf_op jit(solution)/shard_map/ppermute | solution.py:365
  4.0 11.2 %collective-permute-start.1 = (bf16[256,512]{1,0:T(8,128)(2,1)S(1)}, bf16[256,512]{1,0:T(8,128)(2,1)S(1)}, u32[]{:S(2)}, u32[]{:S(2)}) collective-permute-start(bf16[256,512]{1,0:T(8,128)(2,1)S(1)} %get-tuple-element.29.refs_0_), channel_id=1, source_target_pairs={{0,1},{1,0},{2,3},{3,2},{4,5},{5,4},{6,7},{7,6},{8,9},{9,8},{10,11... | collective-permute-start | bytes 786440 | tf_op jit(solution)/shard_map/ppermute | solution.py:354
  4.6 9.8 %collective-permute-start.2 = (bf16[512,128]{1,0:T(8,128)(2,1)}, bf16[512,128]{1,0:T(8,128)(2,1)S(1)}, u32[]{:S(2)}, u32[]{:S(2)}) collective-permute-start(bf16[512,128]{1,0:T(8,128)(2,1)} %bitcast.13), channel_id=1, source_target_pairs={{0,1},{1,0},{2,3},{3,2},{4,5},{5,4},{6,7},{7,6},{8,9},{9,8},{10,11... | collective-permute-start | bytes 393224 | tf_op jit(solution)/shard_map/ppermute | solution.py:354
  9.2 6.0 %collective-permute-start.3 = (bf16[512,128]{1,0:T(8,128)(2,1)S(1)}, bf16[512,128]{1,0:T(8,128)(2,1)S(1)}, u32[]{:S(2)}, u32[]{:S(2)}) collective-permute-start(bf16[512,128]{1,0:T(8,128)(2,1)S(1)} %collective-permute-done.refs_1_.refs_4_), channel_id=1, source_target_pairs={{0,1},{1,0},{2,3},{3,2},{4,5},{5,4},{6,7},{7,6},{8,9},{9,8},{10,11... | collective-permute-start | bytes 393224 | tf_op jit(solution)/shard_map/ppermute | solution.py:354
  13.8 1.4 %collective-permute-start.4 = (f32[36,256]{1,0:T(8,128)S(1)}, f32[36,256]{1,0:T(8,128)S(1)}, u32[]{:S(2)}, u32[]{:S(2)}) collective-permute-start(f32[36,256]{1,0:T(8,128)S(1)} %get-tuple-element.30.refs_6_), channel_id=1, source_target_pairs={{0,1},{1,0},{2,3},{3,2},{4,5},{5,4},{6,7},{7,6},{8,9},{9,8},{10,11... | collective-permute-start | bytes 110600 | tf_op jit(solution)/shard_map/ppermute | solution.py:354

commit v2 on v0

--- a/solution.py
+++ b/solution.py
@@ -61,10 +61,6 @@
 
 def shaped(shape, kind=f32):
     return jax.ShapeDtypeStruct(shape, kind)
-
-
-def paired(place, turn, size):
-    return place ^ turn if size & (size - 1) == 0 else (place + turn) % size
 
 
 def cell_matrix(height, width, cells):
@@ -171,10 +167,16 @@
     shift_pool = exact(cells, pooled_shift, COLS_COLS)
     norm_pool = exact(cells, pooled_norm, COLS_COLS)
     scale_pool = norm_pool * gamma[...] + shift_pool * beta[...]
-    small[0:depth] = exact(lat, scale_pool, ROWS_COLS)
-    small[depth:2 * depth] = exact(lat, shift_pool, ROWS_COLS)
-    for row, field in enumerate((norm_pool * tab[...], shift_pool * tab[...], scale_pool, shift_pool)):
-        small[2 * depth + row:2 * depth + row + 1] = jnp.sum(field, axis=0, keepdims=True)
+    parts = [exact(lat, scale_pool, ROWS_COLS), exact(lat, shift_pool, ROWS_COLS)]
+    for field in (norm_pool * tab[...], shift_pool * tab[...], scale_pool, shift_pool):
+        parts.append(jnp.sum(field, axis=0, keepdims=True))
+    lanes = small.shape[1]
+    small[small.shape[0] - TILE:] = jnp.zeros((TILE, lanes), f32)
+    at = 0
+    for k in range(chans // lanes):
+        for part in parts:
+            small[at:at + part.shape[0]] = part[:, k * lanes:(k + 1) * lanes]
+            at += part.shape[0]
     latent_sum = exact(scale_pool, ws[...], ROWS_ROWS) + exact(shift_pool, wt[...], ROWS_ROWS)
     first, second = latent_sum[:length // 2], latent_sum[length // 2:]
     even = device % 2 == 0
@@ -186,9 +188,7 @@
     acts, refs = refs[:videos], refs[videos:]
     grads, refs = refs[:videos], refs[videos:]
     beyond, refs = refs[:videos], refs[videos:]
-    smalls, refs = refs[:videos], refs[videos:]
-    lat_far, own, refs = refs[0], refs[1], refs[2:]
-    sends, small_out, packs, blocks = refs[:near - 1], refs[near - 1], refs[near], refs[near + 1]
+    own_far, own_line, line_send, *sends, packs, blocks = refs
     pixels = height * width
     chans = acts[0].shape[0]
     lanes = grads[0].shape[1]
@@ -198,11 +198,6 @@
     per = min(videos, TAPS)
     banks = -(-TAPS // per)
     lane = lax.broadcasted_iota(jnp.int32, (1, lanes), 1)
-    small = functools.reduce(lambda a, b: a + b, [ref[...] for ref in smalls])
-    small_out[...] = jnp.zeros_like(small_out)
-    for k in range(chans // lanes):
-        small_out[k * small.shape[0]:(k + 1) * small.shape[0]] = small[:, k * lanes:(k + 1) * lanes]
-
     clear_borders(packs, width)
     for video in range(videos):
         for half, source in enumerate((grads[video], beyond[video])):
@@ -268,66 +263,69 @@
                     extra = extra + dot(firsts, right, ROWS_COLS)
                 put(extra, True)
 
-    me = device % near
-    own[...] = blocks[:, me]
-    top, rest = halves(small_out[...])
-    count = top.shape[0]
+    line, place = device // near, device % near
+    own_line[...] = blocks[line]
+    for k in range(near):
+        line_send[k * piece:(k + 1) * piece] = blocks[line ^ 1, k].astype(bf16)
+    for k in range(far - 2):
+        own_far[k] = blocks[line ^ (k + 2), place]
+        for turn, send in enumerate(sends, 1):
+            send[k * piece:(k + 1) * piece] = blocks[line ^ (k + 2), place ^ turn].astype(bf16)
+
+
+def first_sum_body(near, far, videos, *refs):
+    own_far, own_line, line_got, refs = refs[0], refs[1], refs[2], refs[3:]
+    plane_got, refs = refs[:near - 1], refs[near - 1:]
+    smalls, lat_far, refs = refs[:videos], refs[videos], refs[videos + 1:]
+    kept, small_out, refs = refs[0], refs[1], refs[2:]
+    plane_sends, line_sends, total = refs[:near - 1], refs[near - 1:-1], refs[-1]
+    piece = own_line.shape[1]
+    count = smalls[0].shape[0]
+    place = lax.axis_index("ctx") % near
+    for k, send in enumerate(line_sends):
+        send[...] = functools.reduce(
+            lambda a, b: a + b[k * piece:(k + 1) * piece].astype(f32), plane_got, own_far[k]).astype(bf16)
+    for k in range(near):
+        total[k] = own_line[k] + line_got[k * piece:(k + 1) * piece].astype(f32)
+    kept[...] = total[place]
+    summed = functools.reduce(lambda a, b: a + b, [ref[...] for ref in smalls])
+    small_out[...] = summed
+    top, rest = halves(summed)
     lat_top, lat_rest = halves(lat_far[...])
     cells, depth = lat_top.shape
-    for turn, send in enumerate(sends, 1):
-        for k in range(far):
-            send[k * piece:(k + 1) * piece] = blocks[k, paired(me, turn, near)].astype(bf16)
-        at = far * piece
-        send[at:at + count] = top
-        send[at + count:at + 2 * count] = rest
-        send[at + 2 * count:at + 2 * count + cells, :depth] = lat_top
-        send[at + 2 * count + cells:at + 2 * count + 2 * cells, :depth] = lat_rest
-
-
-def plane_sum_body(near, far, *refs):
-    own, got, small, lat_own = refs[0], refs[1:near], refs[near], refs[near + 1]
-    kept, sends, small_out, latent_grad, total = (
-        refs[near + 2], refs[near + 3:near + far + 2], *refs[near + far + 2:])
-    piece = own.shape[1]
+    at = piece + 2 * count
+    for turn, send in enumerate(plane_sends, 1):
+        send[0:piece] = total[place ^ turn].astype(bf16)
+        send[piece:piece + count] = top
+        send[piece + count:at] = rest
+        send[at:at + cells, :depth] = lat_top
+        send[at + cells:at + 2 * cells, :depth] = lat_rest
+
+
+def last_sum_body(near, far, *refs):
+    kept, small, lat_own, refs = refs[0], refs[1], refs[2], refs[3:]
+    plane_got, line_got, refs = refs[:near - 1], refs[near - 1:near + far - 3], refs[near + far - 3:]
+    filter_grad, mod_grads, vector_grads, latent_grad = refs
+    piece, lanes = kept.shape
     count = small.shape[0]
-    cells, depth = lat_own.shape
-    for k in range(far):
-        total[k] = functools.reduce(lambda a, b: a + b[k * piece:(k + 1) * piece].astype(f32), got, own[k])
-    at = far * piece
 
     def joined(ref, start, length):
         return ref[start:start + length].astype(f32) + ref[start + length:start + 2 * length].astype(f32)
 
-    summed = functools.reduce(lambda a, b: a + joined(b, at, count), got, small[...])
-    small_out[...] = summed
-    latent_grad[...] = lat_own[...] + joined(got[0], at + 2 * count, cells)[:, :depth]
-    me = lax.axis_index("ctx") // near
-    kept[...] = total[me]
-    top, rest = halves(summed)
-    for turn, send in enumerate(sends, 1):
-        send[0:piece] = total[paired(me, turn, far)].astype(bf16)
-        send[piece:piece + count] = top
-        send[piece + count:piece + 2 * count] = rest
-
-
-def line_sum_body(far, *refs):
-    kept, got, small, filter_grad, mod_grads, vector_grads = refs[0], refs[1:far], *refs[far:]
-    piece, lanes = kept.shape
-    count = small.shape[0]
-    total = functools.reduce(lambda a, b: a + b[0:piece].astype(f32), got, kept[...])
+    total = functools.reduce(lambda a, b: a + b[0:piece].astype(f32), plane_got + line_got, kept[...])
     cols, rows = filter_grad.shape
     turned = total.T
     for part in range(lanes // cols):
         first, last = part * piece, min(rows, (part + 1) * piece)
         if first < last:
             filter_grad[:, first:last] = turned[part * cols:(part + 1) * cols, :last - first]
-    summed = functools.reduce(
-        lambda a, b: a + b[piece:piece + count].astype(f32) + b[piece + count:piece + 2 * count].astype(f32),
-        got, small[...])
+    summed = functools.reduce(lambda a, b: a + joined(b, piece, count), plane_got, small[...])
     split, length = mod_grads.shape[0], mod_grads.shape[0] + vector_grads.shape[0]
     for k in range(mod_grads.shape[1] // lanes):
         mod_grads[:, k * lanes:(k + 1) * lanes] = summed[k * length:k * length + split]
         vector_grads[:, k * lanes:(k + 1) * lanes] = summed[k * length + split:(k + 1) * length]
+    cells, depth = lat_own.shape
+    latent_grad[...] = lat_own[...] + joined(plane_got[0], piece + 2 * count, cells)[:, :depth]
 
 
 def local(features, grad_out, mean, rstd, latent, gamma, beta, ws, bs, wt, bt, kernel):
@@ -353,13 +351,11 @@
             lax.ppermute(value, "vid", [(s, (s + turn) % videos) for s in range(videos)])
             for turn in range(1, videos)]
 
-    def near_got(values):
-        return [along_ctx(value, lambda s: s - s % near + paired(s % near, turn, near))
-                for turn, value in enumerate(values, 1)]
-
-    def far_got(values):
-        return [along_ctx(value, lambda s: paired(s // near, turn, far) * near + s % near)
-                for turn, value in enumerate(values, 1)]
+    def plane_got(values):
+        return [along_ctx(value, lambda s: s ^ turn) for turn, value in enumerate(values, 1)]
+
+    def line_got(values, first):
+        return [along_ctx(value, lambda s: s ^ (turn * near)) for turn, value in enumerate(values, first)]
 
     beyond = lax.ppermute(grads, "ctx", [(s, s - 1) for s in range(1, count)])
     act_t, slope, normed, gain, tab = call(
@@ -370,39 +366,39 @@
         far_args=tuple(range(10)),
     )(feats, mean, rstd, latent, gamma, beta, ws, bs, wt, bt)
     grads_all, acts_all, beyond_all = others(grads), others(act_t), others(beyond)
-    small_rows = 2 * depth + 4
     cells = length // 2
+    count_small = -(-(2 * depth + 4) * (chans // outs) // TILE) * TILE
     feats_grad, small, lat_own, lat_far = call(
         functools.partial(input_grad_body, frames, height, width),
-        (shaped((size, chans), bf16), shaped((small_rows, chans)), shaped((cells, depth)), shaped((cells, depth))),
+        (shaped((size, chans), bf16), shaped((count_small, outs)), shaped((cells, depth)), shaped((cells, depth))),
         (pltpu.VMEM((TAPS, 2 * frames, (height + 2) * width, outs), bf16), pltpu.VMEM((size, chans), f32)),
         name="input_grad",
         far_args=(0, 2, 7, 8, 9, 10, 11),
     )(grads, beyond, kernel, slope, normed, gain, tab, latent, ws, wt, gamma, beta)
+    small = functools.reduce(lambda a, b: a + b, line_got([small] * (far - 1), 1), small)
     banks = -(-TAPS // min(videos, TAPS))
-    count_small = -(-small_rows * (chans // outs) // TILE) * TILE
-    extra = 2 * count_small + -(-2 * cells // TILE) * TILE
-    own, *sends, small = call(
+    own_far, own_line, line_send, *plane_sends = call(
         functools.partial(filter_grad_body, frames, height, width, videos, near, piece),
-        [shaped((far, piece, outs))] + [shaped((far * piece + extra, outs), bf16)] * (near - 1)
-        + [shaped((count_small, outs))],
+        [shaped((far - 2, piece, outs)), shaped((near, piece, outs)), shaped((near * piece, outs), bf16)]
+        + [shaped(((far - 2) * piece, outs), bf16)] * (near - 1),
         (pltpu.VMEM((videos, banks, 2 * frames, (height + 2) * width, outs), bf16),
          pltpu.VMEM((far, near, piece, outs), f32)),
         name="filter_grad",
         far_args=(videos,),
-    )(*acts_all, *grads_all, *beyond_all, *others(small), lat_far)
-    kept, *sends, small, latent_grad = call(
-        functools.partial(plane_sum_body, near, far),
-        [shaped((piece, outs))] + [shaped((piece + 2 * count_small, outs), bf16)] * (far - 1)
-        + [shaped((count_small, outs)), shaped((cells, depth))],
-        (pltpu.VMEM((far, piece, outs), f32),),
-        name="plane_sum",
-    )(own, *near_got(sends), small, lat_own)
-    filter_grad, mod_grads, vector_grads = call(
-        functools.partial(line_sum_body, far),
-        (shaped((cols, rows)), shaped((2 * depth, chans)), shaped((4, chans))),
-        name="line_sum",
-    )(kept, *far_got(sends), small)
+    )(*acts_all, *grads_all, *beyond_all)
+    extra = 2 * count_small + -(-2 * cells // TILE) * TILE
+    kept, small, *sends = call(
+        functools.partial(first_sum_body, near, far, videos),
+        [shaped((piece, outs)), shaped((count_small, outs))]
+        + [shaped((piece + extra, outs), bf16)] * (near - 1) + [shaped((piece, outs), bf16)] * (far - 2),
+        (pltpu.VMEM((near, piece, outs), f32),),
+        name="first_sum",
+    )(own_far, own_line, *line_got([line_send], 1), *plane_got(plane_sends), *others(small), lat_far)
+    filter_grad, mod_grads, vector_grads, latent_grad = call(
+        functools.partial(last_sum_body, near, far),
+        (shaped((cols, rows)), shaped((2 * depth, chans)), shaped((4, chans)), shaped((cells, depth))),
+        name="last_sum",
+    )(kept, small, lat_own, *plane_got(sends[:near - 1]), *line_got(sends[near - 1:], 2))
     return (
         feats_grad.reshape(features.shape),
         filter_grad.T,

time: 49.2 us -> 45.1 us (0.917)
  waiting for transfers between devices: 25.2 us -> 14.6 us
  starting transfers between devices: 10.4 us -> 17.6 us
  Pallas kernels: 12.8 us -> 12 us
    ppermute x6 -> x12, waiting for transfers between devices: 19.7 us -> 8.8 us  [along_ctx(): return lax.ppermute(value, 'ctx', [(s, target(s)) for s in range(count)])]
    ppermute x6 -> x12, starting transfers between devices: 7.94 us -> 15.7 us  [along_ctx(): return lax.ppermute(value, 'ctx', [(s, target(s)) for s in range(count)])]
    pallas_call x5, Pallas kernels: 12.8 us -> 12 us  [run(): pl.pallas_call(full if far_args else body, out_shape=outs, in_specs=[pl.B...]
  transfers between devices with their start and end apart: 11 -> 17, of which waited for: 6 -> 7; matrix products, arithmetic and copies ran while one was open for 0% -> 0% of each run, Pallas kernels for 14% -> 25%
where the time goes in v2:
time: 45.1 us; the launch traced here: 44.9 us
  starting transfers between devices  17.6 us (39%)
  waiting for transfers between devices  14.6 us (32%)
  Pallas kernels  12 us (27%)
  between operations  0.71 us (2%)
    ppermute x12, starting transfers between devices, along_ctx(): return lax.ppermute(value, 'ctx', [(s, target(s)) for s in range(count)])  15.7 us
    pallas_call x5, Pallas kernels, run(): pl.pallas_call(full if far_args else body, out_shape=outs, in_specs=[pl.B...  12 us
    ppermute x12, waiting for transfers between devices, along_ctx(): return lax.ppermute(value, 'ctx', [(s, target(s)) for s in range(count)])  8.8 us
    ppermute x1, waiting for transfers between devices, local(): beyond = lax.ppermute(grads, 'ctx', [(s, s - 1) for s in range(1, count)])  4.55 us
    ppermute x1, starting transfers between devices, local(): beyond = lax.ppermute(grads, 'ctx', [(s, s - 1) for s in range(1, count)])  1.29 us
    ppermute x4, waiting for transfers between devices, others(): lax.ppermute(value, 'vid', [(s, (s + turn) % videos) for s in range(video...  1.21 us
  transfers between devices with their start and end apart: 17, of which 7 were waited for; matrix products, arithmetic and copies ran while one was open for 0% of the time, Pallas kernels for 25%

profile of v2, /device:TPU:0, one launch (start us, length us, event | category | flops | bytes accessed | tf_op | source)
XLA Modules:
  0.0 44.9 jit_solution(15689201443401102814)
XLA Ops:
  0.6 1.3 %collective-permute-start = (bf16[512,128]{1,0:T(8,128)(2,1)}, bf16[512,128]{1,0:T(8,128)(2,1)S(1)}, u32[]{:S(2)}, u32[]{:S(2)}) collective-permute-start(bf16[512,128]{1,0:T(8,128)(2,1)} %bitcast.12), channel_id=1, source_target_pairs={{2,0},{4,2},{6,4},{8,6},{10,8},{12,10},{14,12},{16,14},{18,16},{20... | collective-permute-start | bytes 393224 | tf_op jit(solution)/shard_map/ppermute | solution.py:360
  1.9 2.1 %modulate.1 = (bf16[256,512]{1,0:T(8,128)(2,1)S(1)}, f32[512,256]{1,0:T(8,128)S(1)}, f32[512,256]{1,0:T(8,128)S(1)}, f32[256,256]{1,0:T(8,128)S(1)}, f32[16,256]{1,0:T(8,128)S(1)}) custom-call(bf16[512,256]{1,0:T(8,128)(2,1)} %bitcast.16, f32[1,32]{1,0:T(1,128)} %refs_1_.1, f32[1,32]{1,0:T(1,128)} %refs_2_.2, f32[1,8,16,16]{3,2,1,0:T(8,128)} %refs_7_.1, ...), custom_call_target="tpu_custom_call" | custom-call | tf_op jit(solution)/shard_map/modulate/pallas_call | solution.py:44
  4.0 0.5 %collective-permute-start.1 = (bf16[256,512]{1,0:T(8,128)(2,1)S(1)}, bf16[256,512]{1,0:T(8,128)(2,1)S(1)}, u32[]{:S(2)}, u32[]{:S(2)}) collective-permute-start(bf16[256,512]{1,0:T(8,128)(2,1)S(1)} %get-tuple-element.36.refs_0_), channel_id=1, source_target_pairs={{0,1},{1,0},{2,3},{3,2},{4,5},{5,4},{6,7},{7,6},{8,9},{9,8},{10,11... | collective-permute-start | bytes 786440 | tf_op jit(solution)/shard_map/ppermute | solution.py:351
  4.6 0.1 collective-permute-start.2
  4.6 4.5 %collective-permute-done.refs_1_.refs_4_ = bf16[512,128]{1,0:T(8,128)(2,1)S(1)} collective-permute-done((bf16[512,128]{1,0:T(8,128)(2,1)}, bf16[512,128]{1,0:T(8,128)(2,1)S(1)}, u32[]{:S(2)}, u32[]{:S(2)}) %collective-permute-start) | collective-permute-done | bytes 131104 | tf_op jit(solution)/shard_map/ppermute | solution.py:360
  9.2 0.0 collective-permute-start.3
  9.2 4.4 %input_grad.1 = (bf16[512,256]{1,0:T(8,128)(2,1)}, f32[80,128]{1,0:T(8,128)S(1)}, f32[8,16]{1,0:T(8,128)S(1)}, f32[8,16]{1,0:T(8,128)S(1)}) custom-call(bf16[512,128]{1,0:T(8,128)(2,1)} %bitcast.14, bf16[512,128]{1,0:T(8,128)(2,1)S(1)} %collective-permute-done.refs_1_.refs_4_, bf16[6912,128]{1,0:T(8,128)(2,1)} %refs_2_.3, ...), custom_call_target="tpu_custom_call" | custom-call | tf_op jit(solution)/shard_map/input_grad/pallas_call | solution.py:44
  13.6 3.2 %collective-permute-start.10 = (f32[80,128]{1,0:T(8,128)S(1)}, f32[80,128]{1,0:T(8,128)S(1)}, u32[]{:S(2)}, u32[]{:S(2)}) collective-permute-start(f32[80,128]{1,0:T(8,128)S(1)} %get-tuple-element.43), channel_id=1, source_target_pairs={{0,24},{2,26},{4,28},{6,30},{8,16},{10,18},{12,20},{14,22},{16,8},... | collective-permute-start | bytes 122888 | tf_op jit(solution)/shard_map/ppermute | solution.py:347
  16.8 0.0 collective-permute-start.9
  16.8 1.2 %collective-permute-start.8 = (f32[80,128]{1,0:T(8,128)S(1)}, f32[80,128]{1,0:T(8,128)S(1)}, u32[]{:S(2)}, u32[]{:S(2)}) collective-permute-start(f32[80,128]{1,0:T(8,128)S(1)} %get-tuple-element.43), channel_id=1, source_target_pairs={{0,8},{2,10},{4,12},{6,14},{8,0},{10,2},{12,4},{14,6},{16,24},{18,... | collective-permute-start | bytes 122888 | tf_op jit(solution)/shard_map/ppermute | solution.py:347
  18.0 0.0 collective-permute-done.1.refs_1_
  18.0 0.0 collective-permute-done.3.refs_5_
  18.0 4.5 %filter_grad.1 = (f32[2,224,128]{2,1,0:T(8,128)S(1)}, f32[4,224,128]{2,1,0:T(8,128)S(1)}, bf16[896,128]{1,0:T(8,128)(2,1)S(1)}, bf16[448,128]{1,0:T(8,128)(2,1)S...) custom-call(bf16[256,512]{1,0:T(8,128)(2,1)S(1)} %get-tuple-element.36.refs_0_, ...), custom_call_target="tpu_custom_call" | custom-call | tf_op jit(solution)/shard_map/filter_grad/pallas_call | solution.py:44
  22.6 0.1 collective-permute-start.4
  22.7 2.0 %collective-permute-start.5 = (bf16[448,128]{1,0:T(8,128)(2,1)S(1)}, bf16[448,128]{1,0:T(8,128)(2,1)S(1)}, u32[]{:S(2)}, u32[]{:S(2)}) collective-permute-start(bf16[448,128]{1,0:T(8,128)(2,1)S(1)} %get-tuple-element.40), channel_id=1, source_target_pairs={{0,2},{2,0},{4,6},{6,4},{8,10},{10,8},{12,14},{14,12},{16,18},{18,... | collective-permute-start | bytes 344072 | tf_op jit(solution)/shard_map/ppermute | solution.py:347
  24.7 0.0 collective-permute-done.10
  24.7 1.9 %collective-permute-start.6 = (bf16[448,128]{1,0:T(8,128)(2,1)S(1)}, bf16[448,128]{1,0:T(8,128)(2,1)S(1)}, u32[]{:S(2)}, u32[]{:S(2)}) collective-permute-start(bf16[448,128]{1,0:T(8,128)(2,1)S(1)} %get-tuple-element.41), channel_id=1, source_target_pairs={{0,4},{2,6},{4,0},{6,2},{8,12},{10,14},{12,8},{14,10},{16,20},{18,... | collective-permute-start | bytes 344072 | tf_op jit(solution)/shard_map/ppermute | solution.py:347
  26.5 0.0 collective-permute-done.9
  26.6 0.1 collective-permute-start.11
  26.6 1.2 %collective-permute-done.11.refs_7_ = f32[80,128]{1,0:T(8,128)S(1)} collective-permute-done((f32[80,128]{1,0:T(8,128)S(1)}, f32[80,128]{1,0:T(8,128)S(1)}, u32[]{:S(2)}, u32[]{:S(2)}) %collective-permute-start.11) | collective-permute-done | bytes 40992 | tf_op jit(solution)/shard_map/ppermute | solution.py:351
  27.9 0.4 collective-permute-done.5.refs_3_
  28.2 2.5 %collective-permute-done.6.refs_4_ = bf16[448,128]{1,0:T(8,128)(2,1)S(1)} collective-permute-done((bf16[448,128]{1,0:T(8,128)(2,1)S(1)}, bf16[448,128]{1,0:T(8,128)(2,1)S(1)}, u32[]{:S(2)}, u32[]{:S(2)}) %collective-permute-start.6) | collective-permute-done | bytes 114720 | tf_op jit(solution)/shard_map/ppermute | solution.py:347
  30.7 1.5 %collective-permute-done.7.refs_5_ = bf16[448,128]{1,0:T(8,128)(2,1)S(1)} collective-permute-done((bf16[448,128]{1,0:T(8,128)(2,1)S(1)}, bf16[448,128]{1,0:T(8,128)(2,1)S(1)}, u32[]{:S(2)}, u32[]{:S(2)}) %collective-permute-start.7) | collective-permute-done | bytes 114720 | tf_op jit(solution)/shard_map/ppermute | solution.py:347
  32.2 0.1 first_sum.1
  32.4 0.7 %collective-permute-start.12 = (bf16[400,128]{1,0:T(8,128)(2,1)S(1)}, bf16[400,128]{1,0:T(8,128)(2,1)S(1)}, u32[]{:S(2)}, u32[]{:S(2)}) collective-permute-start(bf16[400,128]{1,0:T(8,128)(2,1)S(1)} %get-tuple-element.48), channel_id=1, source_target_pairs={{0,2},{2,0},{4,6},{6,4},{8,10},{10,8},{12,14},{14,12},{16,18},{18,... | collective-permute-start | bytes 307208 | tf_op jit(solution)/shard_map/ppermute | solution.py:347
  33.1 0.7 %collective-permute-start.13 = (bf16[400,128]{1,0:T(8,128)(2,1)S(1)}, bf16[400,128]{1,0:T(8,128)(2,1)S(1)}, u32[]{:S(2)}, u32[]{:S(2)}) collective-permute-start(bf16[400,128]{1,0:T(8,128)(2,1)S(1)} %get-tuple-element.49), channel_id=1, source_target_pairs={{0,4},{2,6},{4,0},{6,2},{8,12},{10,14},{12,8},{14,10},{16,20},{18,... | collective-permute-start | bytes 307208 | tf_op jit(solution)/shard_map/ppermute | solution.py:347
  33.8 2.1 %collective-permute-start.14 = (bf16[400,128]{1,0:T(8,128)(2,1)S(1)}, bf16[400,128]{1,0:T(8,128)(2,1)S(1)}, u32[]{:S(2)}, u32[]{:S(2)}) collective-permute-start(bf16[400,128]{1,0:T(8,128)(2,1)S(1)} %get-tuple-element.50), channel_id=1, source_target_pairs={{0,6},{2,4},{4,2},{6,0},{8,14},{10,12},{12,10},{14,8},{16,22},{18,... | collective-permute-start | bytes 307208 | tf_op jit(solution)/shard_map/ppermute | solution.py:347
  35.9 2.2 %collective-permute-start.15 = (bf16[224,128]{1,0:T(8,128)(2,1)S(1)}, bf16[224,128]{1,0:T(8,128)(2,1)S(1)}, u32[]{:S(2)}, u32[]{:S(2)}) collective-permute-start(bf16[224,128]{1,0:T(8,128)(2,1)S(1)} %get-tuple-element.51), channel_id=1, source_target_pairs={{0,16},{2,18},{4,20},{6,22},{8,24},{10,26},{12,28},{14,30},{16,0},... | collective-permute-start | bytes 172040 | tf_op jit(solution)/shard_map/ppermute | solution.py:347
  38.1 1.6 %collective-permute-start.16 = (bf16[224,128]{1,0:T(8,128)(2,1)S(1)}, bf16[224,128]{1,0:T(8,128)(2,1)S(1)}, u32[]{:S(2)}, u32[]{:S(2)}) collective-permute-start(bf16[224,128]{1,0:T(8,128)(2,1)S(1)} %get-tuple-element.52), channel_id=1, source_target_pairs={{0,24},{2,26},{4,28},{6,30},{8,16},{10,18},{12,20},{14,22},{16,8},... | collective-permute-start | bytes 172040 | tf_op jit(solution)/shard_map/ppermute | solution.py:347
  39.7 1.3 %collective-permute-done.15.refs_6_ = bf16[224,128]{1,0:T(8,128)(2,1)S(1)} collective-permute-done((bf16[224,128]{1,0:T(8,128)(2,1)S(1)}, bf16[224,128]{1,0:T(8,128)(2,1)S(1)}, u32[]{:S(2)}, u32[]{:S(2)}) %collective-permute-start.15) | collective-permute-done | bytes 57376 | tf_op jit(solution)/shard_map/ppermute | solution.py:347
  41.0 3.1 %collective-permute-done.16.refs_7_ = bf16[224,128]{1,0:T(8,128)(2,1)S(1)} collective-permute-done((bf16[224,128]{1,0:T(8,128)(2,1)S(1)}, bf16[224,128]{1,0:T(8,128)(2,1)S(1)}, u32[]{:S(2)}, u32[]{:S(2)}) %collective-permute-start.16) | collective-permute-done | bytes 57376 | tf_op jit(solution)/shard_map/ppermute | solution.py:347
  44.1 0.8 %last_sum.1 = (f32[64,432]{1,0:T(8,128)}, f32[32,256]{1,0:T(8,128)}, f32[4,256]{1,0:T(4,128)}, f32[8,16]{1,0:T(8,128)}) custom-call(f32[224,128]{1,0:T(8,128)S(1)} %get-tuple-element.45.refs_0_, f32[80,128]{1,0:T(8,128)S(1)} %get-tuple-element.46.refs_1_, f32[8,16]{1,0:T(8,128)S(1)} %get-tuple-element.47.refs_2_, ...), custom_call_target="tpu_custom_call" | custom-call | tf_op jit(solution)/shard_map/last_sum/pallas_call | solution.py:44
  (8 shorter events, 0.0 us)
Async XLA Ops:
  0.6 8.5 %collective-permute-start = (bf16[512,128]{1,0:T(8,128)(2,1)}, bf16[512,128]{1,0:T(8,128)(2,1)S(1)}, u32[]{:S(2)}, u32[]{:S(2)}) collective-permute-start(bf16[512,128]{1,0:T(8,128)(2,1)} %bitcast.12), channel_id=1, source_target_pairs={{2,0},{4,2},{6,4},{8,6},{10,8},{12,10},{14,12},{16,14},{18,16},{20... | collective-permute-start | bytes 393224 | tf_op jit(solution)/shard_map/ppermute | solution.py:360
  4.0 14.0 %collective-permute-start.1 = (bf16[256,512]{1,0:T(8,128)(2,1)S(1)}, bf16[256,512]{1,0:T(8,128)(2,1)S(1)}, u32[]{:S(2)}, u32[]{:S(2)}) collective-permute-start(bf16[256,512]{1,0:T(8,128)(2,1)S(1)} %get-tuple-element.36.refs_0_), channel_id=1, source_target_pairs={{0,1},{1,0},{2,3},{3,2},{4,5},{5,4},{6,7},{7,6},{8,9},{9,8},{10,11... | collective-permute-start | bytes 786440 | tf_op jit(solution)/shard_map/ppermute | solution.py:351
  4.6 12.2 %collective-permute-start.2 = (bf16[512,128]{1,0:T(8,128)(2,1)}, bf16[512,128]{1,0:T(8,128)(2,1)S(1)}, u32[]{:S(2)}, u32[]{:S(2)}) collective-permute-start(bf16[512,128]{1,0:T(8,128)(2,1)} %bitcast.13), channel_id=1, source_target_pairs={{0,1},{1,0},{2,3},{3,2},{4,5},{5,4},{6,7},{7,6},{8,9},{9,8},{10,11... | collective-permute-start | bytes 393224 | tf_op jit(solution)/shard_map/ppermute | solution.py:351
  9.2 8.9 %collective-permute-start.3 = (bf16[512,128]{1,0:T(8,128)(2,1)S(1)}, bf16[512,128]{1,0:T(8,128)(2,1)S(1)}, u32[]{:S(2)}, u32[]{:S(2)}) collective-permute-start(bf16[512,128]{1,0:T(8,128)(2,1)S(1)} %collective-permute-done.refs_1_.refs_4_), channel_id=1, source_target_pairs={{0,1},{1,0},{2,3},{3,2},{4,5},{5,4},{6,7},{7,6},{8,9},{9,8},{10,11... | collective-permute-start | bytes 393224 | tf_op jit(solution)/shard_map/ppermute | solution.py:351
  13.6 11.1 %collective-permute-start.10 = (f32[80,128]{1,0:T(8,128)S(1)}, f32[80,128]{1,0:T(8,128)S(1)}, u32[]{:S(2)}, u32[]{:S(2)}) collective-permute-start(f32[80,128]{1,0:T(8,128)S(1)} %get-tuple-element.43), channel_id=1, source_target_pairs={{0,24},{2,26},{4,28},{6,30},{8,16},{10,18},{12,20},{14,22},{16,8},... | collective-permute-start | bytes 122888 | tf_op jit(solution)/shard_map/ppermute | solution.py:347
  16.8 9.7 %collective-permute-start.9 = (f32[80,128]{1,0:T(8,128)S(1)}, f32[80,128]{1,0:T(8,128)S(1)}, u32[]{:S(2)}, u32[]{:S(2)}) collective-permute-start(f32[80,128]{1,0:T(8,128)S(1)} %get-tuple-element.43), channel_id=1, source_target_pairs={{0,16},{2,18},{4,20},{6,22},{8,24},{10,26},{12,28},{14,30},{16,0},... | collective-permute-start | bytes 122888 | tf_op jit(solution)/shard_map/ppermute | solution.py:347
  16.8 9.7 %collective-permute-start.8 = (f32[80,128]{1,0:T(8,128)S(1)}, f32[80,128]{1,0:T(8,128)S(1)}, u32[]{:S(2)}, u32[]{:S(2)}) collective-permute-start(f32[80,128]{1,0:T(8,128)S(1)} %get-tuple-element.43), channel_id=1, source_target_pairs={{0,8},{2,10},{4,12},{6,14},{8,0},{10,2},{12,4},{14,6},{16,24},{18,... | collective-permute-start | bytes 122888 | tf_op jit(solution)/shard_map/ppermute | solution.py:347
  22.6 9.6 %collective-permute-start.4 = (bf16[896,128]{1,0:T(8,128)(2,1)S(1)}, bf16[896,128]{1,0:T(8,128)(2,1)S(1)}, u32[]{:S(2)}, u32[]{:S(2)}) collective-permute-start(bf16[896,128]{1,0:T(8,128)(2,1)S(1)} %get-tuple-element.39), channel_id=1, source_target_pairs={{0,8},{2,10},{4,12},{6,14},{8,0},{10,2},{12,4},{14,6},{16,24},{18,... | collective-permute-start | bytes 688136 | tf_op jit(solution)/shard_map/ppermute | solution.py:347
  22.7 5.5 %collective-permute-start.5 = (bf16[448,128]{1,0:T(8,128)(2,1)S(1)}, bf16[448,128]{1,0:T(8,128)(2,1)S(1)}, u32[]{:S(2)}, u32[]{:S(2)}) collective-permute-start(bf16[448,128]{1,0:T(8,128)(2,1)S(1)} %get-tuple-element.40), channel_id=1, source_target_pairs={{0,2},{2,0},{4,6},{6,4},{8,10},{10,8},{12,14},{14,12},{16,18},{18,... | collective-permute-start | bytes 344072 | tf_op jit(solution)/shard_map/ppermute | solution.py:347
  24.7 6.0 %collective-permute-start.6 = (bf16[448,128]{1,0:T(8,128)(2,1)S(1)}, bf16[448,128]{1,0:T(8,128)(2,1)S(1)}, u32[]{:S(2)}, u32[]{:S(2)}) collective-permute-start(bf16[448,128]{1,0:T(8,128)(2,1)S(1)} %get-tuple-element.41), channel_id=1, source_target_pairs={{0,4},{2,6},{4,0},{6,2},{8,12},{10,14},{12,8},{14,10},{16,20},{18,... | collective-permute-start | bytes 344072 | tf_op jit(solution)/shard_map/ppermute | solution.py:347
  26.5 5.7 %collective-permute-start.7 = (bf16[448,128]{1,0:T(8,128)(2,1)S(1)}, bf16[448,128]{1,0:T(8,128)(2,1)S(1)}, u32[]{:S(2)}, u32[]{:S(2)}) collective-permute-start(bf16[448,128]{1,0:T(8,128)(2,1)S(1)} %get-tuple-element.42), channel_id=1, source_target_pairs={{0,6},{2,4},{4,2},{6,0},{8,14},{10,12},{12,10},{14,8},{16,22},{18,... | collective-permute-start | bytes 344072 | tf_op jit(solution)/shard_map/ppermute | solution.py:347
  26.6 1.3 %collective-permute-start.11 = (f32[80,128]{1,0:T(8,128)S(1)}, f32[80,128]{1,0:T(8,128)S(1)}, u32[]{:S(2)}, u32[]{:S(2)}) collective-permute-start(f32[80,128]{1,0:T(8,128)S(1)} %add_add_fusion.refs_6_), channel_id=1, source_target_pairs={{0,1},{1,0},{2,3},{3,2},{4,5},{5,4},{6,7},{7,6},{8,9},{9,8},{10,11... | collective-permute-start | bytes 122888 | tf_op jit(solution)/shard_map/ppermute | solution.py:351
  32.4 11.7 %collective-permute-start.12 = (bf16[400,128]{1,0:T(8,128)(2,1)S(1)}, bf16[400,128]{1,0:T(8,128)(2,1)S(1)}, u32[]{:S(2)}, u32[]{:S(2)}) collective-permute-start(bf16[400,128]{1,0:T(8,128)(2,1)S(1)} %get-tuple-element.48), channel_id=1, source_target_pairs={{0,2},{2,0},{4,6},{6,4},{8,10},{10,8},{12,14},{14,12},{16,18},{18,... | collective-permute-start | bytes 307208 | tf_op jit(solution)/shard_map/ppermute | solution.py:347
  33.1 11.0 %collective-permute-start.13 = (bf16[400,128]{1,0:T(8,128)(2,1)S(1)}, bf16[400,128]{1,0:T(8,128)(2,1)S(1)}, u32[]{:S(2)}, u32[]{:S(2)}) collective-permute-start(bf16[400,128]{1,0:T(8,128)(2,1)S(1)} %get-tuple-element.49), channel_id=1, source_target_pairs={{0,4},{2,6},{4,0},{6,2},{8,12},{10,14},{12,8},{14,10},{16,20},{18,... | collective-permute-start | bytes 307208 | tf_op jit(solution)/shard_map/ppermute | solution.py:347
  33.8 10.3 %collective-permute-start.14 = (bf16[400,128]{1,0:T(8,128)(2,1)S(1)}, bf16[400,128]{1,0:T(8,128)(2,1)S(1)}, u32[]{:S(2)}, u32[]{:S(2)}) collective-permute-start(bf16[400,128]{1,0:T(8,128)(2,1)S(1)} %get-tuple-element.50), channel_id=1, source_target_pairs={{0,6},{2,4},{4,2},{6,0},{8,14},{10,12},{12,10},{14,8},{16,22},{18,... | collective-permute-start | bytes 307208 | tf_op jit(solution)/shard_map/ppermute | solution.py:347
  35.9 5.1 %collective-permute-start.15 = (bf16[224,128]{1,0:T(8,128)(2,1)S(1)}, bf16[224,128]{1,0:T(8,128)(2,1)S(1)}, u32[]{:S(2)}, u32[]{:S(2)}) collective-permute-start(bf16[224,128]{1,0:T(8,128)(2,1)S(1)} %get-tuple-element.51), channel_id=1, source_target_pairs={{0,16},{2,18},{4,20},{6,22},{8,24},{10,26},{12,28},{14,30},{16,0},... | collective-permute-start | bytes 172040 | tf_op jit(solution)/shard_map/ppermute | solution.py:347
  38.1 6.0 %collective-permute-start.16 = (bf16[224,128]{1,0:T(8,128)(2,1)S(1)}, bf16[224,128]{1,0:T(8,128)(2,1)S(1)}, u32[]{:S(2)}, u32[]{:S(2)}) collective-permute-start(bf16[224,128]{1,0:T(8,128)(2,1)S(1)} %get-tuple-element.52), channel_id=1, source_target_pairs={{0,24},{2,26},{4,28},{6,30},{8,16},{10,18},{12,20},{14,22},{16,8},... | collective-permute-start | bytes 172040 | tf_op jit(solution)/shard_map/ppermute | solution.py:347
